TPU v7x, 128 devices: a whole 4x4x4 slice. The times are simulated.
128 devices in a mesh: row: 8 (over z_hi, y), col: 16 (over z_lo, x, core).
Axes of the slice: x: 4, y: 4, z: 4 (z_hi: 2, z_lo: 2; z = z_hi * 2 + z_lo), core: 2. Of those that a mesh axis runs over, the one named last changes fastest.
Arguments:
- pair: bfloat16 [1024, 1024, 128], P('row', 'col'), may hold values from -6 to 6
- ln_gain: float32 [128], replicated, may hold values from 0.1 to 1.9
- w_query: bfloat16 [128, 128], replicated, may hold values from -21.213203 to 21.213203
- w_key: bfloat16 [128, 128], replicated, may hold values from -0.5 to 0.5
- w_value: bfloat16 [128, 128], replicated, may hold values from -0.5 to 0.5
- w_gate: bfloat16 [128, 128], replicated, may hold values from -0.5 to 0.5
- w_bias: bfloat16 [128, 4], replicated, may hold values from -1.0546875 to 1.0546875
- w_out: bfloat16 [128, 128], replicated, may hold values from -1.5 to 1.5
Outputs:
- update: bfloat16 [1024, 1024, 128], P('row', 'col')
All inputs are finite; a program needn't handle non-finite values.
Results may differ from a plain program's by a relative error of at most 0.009.
The roundings to bfloat16 on the way count: a program that leaves them out, or rounds other values in their place, can miss the bound.
Values may be sent and summed in bfloat16 or wider, within the bound.
A program may use at most 256 MiB of HBM per device.

v0:
```python
import math

import jax
import jax.numpy as jnp
from jax import lax
from jax.sharding import PartitionSpec as P


def from_root(value, axis, root):
    mine = lax.axis_index(axis) == root
    return lax.psum(jnp.where(mine, value, jnp.zeros_like(value)), axis)


def layer_norm(tile, gain):
    values = tile.astype(jnp.float32)
    center = jnp.mean(values, axis=-1, keepdims=True)
    spread = jnp.mean(jnp.square(values - center), axis=-1, keepdims=True)
    return ((values - center) * lax.rsqrt(spread + 1e-05) * gain).astype(jnp.bfloat16)


def split_heads(matrix, heads):
    return matrix.reshape(matrix.shape[:-1] + (heads, matrix.shape[-1] // heads))


def start_state(rows_count, query_count, heads, head_dim):
    most = jnp.full((rows_count, query_count, heads), -1e30, jnp.float32)
    total = jnp.zeros((rows_count, query_count, heads), jnp.float32)
    summed = jnp.zeros((rows_count, query_count, heads, head_dim), jnp.float32)
    return (most, total, summed)


def absorb(carry, query, key_rows, bias_block, w_key, w_value, heads):
    most, total, summed = carry
    keys = split_heads(
        jnp.dot(key_rows, w_key, preferred_element_type=jnp.float32).astype(jnp.bfloat16), heads
    )
    values = split_heads(
        jnp.dot(key_rows, w_value, preferred_element_type=jnp.float32).astype(jnp.bfloat16), heads
    )
    scores = jnp.einsum("abhe,akhe->abhk", query, keys, preferred_element_type=jnp.float32)
    scores = scores + bias_block.astype(jnp.float32)[None]
    newest = jnp.maximum(most, jnp.max(scores, axis=-1))
    factor = jnp.exp(most - newest)
    weights = jnp.exp(scores - newest[..., None])
    total = total * factor + jnp.sum(weights, axis=-1)
    summed = summed * factor[..., None] + jnp.einsum(
        "abhk,akhe->abhe", weights.astype(jnp.bfloat16), values, preferred_element_type=jnp.float32
    )
    return (newest, total, summed)


def sweep(carry, query, key_rows, bias_rows, w_key, w_value, heads):
    count = key_rows.shape[1]
    block = math.gcd(count, 256)
    turns = count // block

    def one_turn(index, state):
        begin = index * block
        rows_part = lax.dynamic_slice_in_dim(key_rows, begin, block, 1)
        bias_part = lax.dynamic_slice_in_dim(bias_rows, begin, block, 2)
        return absorb(state, query, rows_part, bias_part, w_key, w_value, heads)

    return lax.fori_loop(0, turns, one_turn, carry)


def finish(carry, gate, w_out):
    most, total, summed = carry
    attended = summed / total[..., None]
    attended = attended.reshape(
        attended.shape[0], attended.shape[1], attended.shape[2] * attended.shape[3]
    )
    gated = (gate * attended).astype(jnp.bfloat16)
    return jnp.dot(gated, w_out, preferred_element_type=jnp.float32).astype(jnp.bfloat16)


def queries_and_gate(normed, w_query, w_gate, heads, scale):
    query = split_heads(
        (jnp.dot(normed, w_query, preferred_element_type=jnp.float32) * scale).astype(jnp.bfloat16),
        heads,
    )
    gate = jax.nn.sigmoid(jnp.dot(normed, w_gate, preferred_element_type=jnp.float32))
    return (query, gate)


def shards(pair, ln_gain, w_query, w_key, w_value, w_gate, w_bias, w_out):
    heads = w_bias.shape[1]
    head_dim = w_query.shape[1] // heads
    scale = 1.0 / math.sqrt(head_dim)
    rows_dev = pair.shape[0]
    cols_dev = pair.shape[1]
    normed = layer_norm(pair, ln_gain)
    tile_bias = jnp.transpose(
        jnp.dot(normed, w_bias, preferred_element_type=jnp.float32).astype(jnp.bfloat16), (0, 2, 1)
    )
    band = lax.all_gather(tile_bias, "col", axis=2, tiled=True)
    ratio = lax.axis_size("col") // lax.axis_size("row")
    column = lax.axis_index("col")
    owner = column // ratio
    mine = lax.dynamic_slice_in_dim(band, column % ratio * cols_dev, cols_dev, 0)
    bias_rows = from_root(mine, "row", owner)
    query, gate = queries_and_gate(normed, w_query, w_gate, heads, scale)
    initial = start_state(rows_dev, cols_dev, heads, head_dim)
    carry = sweep(
        initial,
        query,
        lax.all_gather(normed, "col", axis=1, tiled=True),
        bias_rows,
        w_key,
        w_value,
        heads,
    )
    return finish(carry, gate, w_out)


def solution(mesh):
    return jax.shard_map(
        shards,
        mesh=mesh,
        in_specs=(P("row", "col", None), P(), P(), P(), P(), P(), P(), P()),
        out_specs=P("row", "col", None),
        check_vma=False,
    )
```

profile of v0, /device:TPU:49, one launch (start us, length us, event | category | flops | bytes accessed | tf_op | source)
XLA Modules:
  0.0 629.9 jit_solution(9313343828444633704)
XLA Ops:
  9.4 4.0 fusion.26
  13.4 5.3 fusion.28
  21.4 34.4 %all-gather.5.cloned.1.call-done = bf16[128,4,1024]{0,1,2:T(4,128)(2,1)} async-done(((bf16[128,4,64]{0,1,2:T(4,128)(2,1)}), bf16[128,4,1024]{0,1,2:T(4,128)(2,1)}) %all-gather.5.cloned.1.call-update) | async-done | bytes 1048592 | tf_op jit(solution)/shard_map/all_gather | solution.py:95
  59.8 3.5 multiply_convert_fusion.1
  63.3 7.9 %copy.22 = bf16[128,64,4,32]{1,3,2,0:T(8,128)(2,1)} copy(bf16[128,64,4,32]{0,3,2,1:T(8,128)(2,1)S(1)} %bitcast.70) | data formatting | bytes 4194304
  71.2 67.1 %all-reduce.2.cloned.1.call-done = bf16[64,4,1024]{0,1,2:T(4,128)(2,1)} async-done(((bf16[64,4,1024]{0,1,2:T(4,128)(2,1)}), bf16[64,4,1024]{0,1,2:T(4,128)(2,1)}) %all-reduce.2.cloned.1.call-update) | async-done | bytes 524304 | tf_op jit(solution)/shard_map/psum | solution.py:11
  140.5 176.7 %all-gather.3.cloned.1.call-done = bf16[128,1024,128]{2,1,0:T(8,128)(2,1)} async-done(((bf16[128,64,128]{2,1,0:T(8,128)(2,1)}), bf16[128,1024,128]{2,1,0:T(8,128)(2,1)}) %all-gather.3.cloned.1.call-update) | async-done | bytes 33554448 | tf_op jit(solution)/shard_map/all_gather | solution.py:106
  317.2 279.5 %while.18 = (s32[]{:T(128)}, f32[128,64,4]{1,2,0:T(4,128)S(1)}, f32[128,64,4]{1,2,0:T(4,128)S(1)}, f32[128,64,4,32]{1,3,2,0:T(8,128)}, bf16[128,1024,128]{2,1,0:...) while((s32[]{:T(128)}, f32[128,64,4]{1,2,0:T(4,128)S(1)}, ...), condition=%wide.region_6.7_spmd.clone, body=%wide.region_3.6_spmd.clone.sunk | while | flops 3300098048 | bytes 164823248 | solution.py:63
  318.1 9.1 %fusion.70 = bf16[128,256,128]{1,2,0:T(8,128)(2,1)} fusion(bf16[128,1024,128]{2,1,0:T(8,128)(2,1)} %get-tuple-element.325, s32[]{:T(128)S(6)} %select_n.39, bf16[128,128]{0,1:T(8,128)(2,1)S(1)} %get-tuple-element.329), kind=kOutput, calls=%fused_computation.15.clone.1 | convolution fusion | flops 1077936128 | bytes 16809988 | tf_op jit(solution)/shard_map/while/body/eval_jaxpr/dot_general | solution.py:38
  327.2 5.7 fusion.66
  332.9 16.0 %fusion.67 = (f32[128,64,4]{1,2,0:T(4,128)S(1)}, f32[128,4,256,64]{2,3,1,0:T(8,128)}) fusion(f32[64,4,256]{2,0,1:T(8,128)S(1)} %dynamic-slice_convert_fusion.2, bf16[128,256,4,32]{1,3,2,0:T(8,128)(2,1)S(1)} %bitcast.68, bf16[128,64,4,32]{1,3,2,0:T(8,128)(2,1)} %get-tuple-element.327), kind=kOutput, calls=%fused_computation.2.clone.1 | convolution fusion | flops 553615360 | bytes 44433408 | tf_op jit(solution)/shard_map/while/body/eval_jaxpr/abhe,akhe->abhk/dot_general | solution.py:40
  349.0 15.6 %fusion.68 = f32[128,64,4]{1,2,0:T(4,128)S(1)} fusion(f32[128,4,256,64]{2,3,1,0:T(8,128)} %get-tuple-element.292, f32[128,64,4]{1,2,0:T(4,128)S(1)} %select_maximum_fusion.2, f32[64,4,256]{2,0,1:T(8,128)S(1)} %dynamic-slice_convert_fusion.2), kind=kLoop, calls=%fused_computation.4.clone.1 | loop fusion | flops 25133056 | bytes 34078720 | tf_op jit(solution)/shard_map/while/body/eval_jaxpr/reduce_sum | solution.py:45
  365.0 20.6 %bitcast_add_fusion.3 = f32[128,64,4,32]{1,3,2,0:T(8,128)} fusion(f32[128,64,4,32]{1,3,2,0:T(8,128)} %get-tuple-element.311, f32[128,64,4]{1,2,0:T(4,128)S(1)} %get-tuple-element.294, pred[]{:T(512)S(6)} %compare.6, bf16[128,256,4,32]{1,3,2,0:T(8,128)(2,1)} %bitcast.67, f32[128,4,256,64]{2,3,1,0:T(8,128)} %get-tuple-element.292, ...), kind=kOutput, calls=%fused_computation.8.clone.1 | convolution fusion | flops 565182464 | bytes 50855936 | tf_op jit(solution)/shard_map/while/body/eval_jaxpr/abhk,akhe->abhe/dot_general | solution.py:46
  386.6 9.1 %fusion.70 = bf16[128,256,128]{1,2,0:T(8,128)(2,1)} fusion(bf16[128,1024,128]{2,1,0:T(8,128)(2,1)} %get-tuple-element.325, s32[]{:T(128)S(6)} %select_n.39, bf16[128,128]{0,1:T(8,128)(2,1)S(1)} %get-tuple-element.329), kind=kOutput, calls=%fused_computation.15.clone.1 | convolution fusion | flops 1077936128 | bytes 16809988 | tf_op jit(solution)/shard_map/while/body/eval_jaxpr/dot_general | solution.py:38
  395.6 5.7 fusion.66
  401.4 16.0 %fusion.67 = (f32[128,64,4]{1,2,0:T(4,128)S(1)}, f32[128,4,256,64]{2,3,1,0:T(8,128)}) fusion(f32[64,4,256]{2,0,1:T(8,128)S(1)} %dynamic-slice_convert_fusion.2, bf16[128,256,4,32]{1,3,2,0:T(8,128)(2,1)S(1)} %bitcast.68, bf16[128,64,4,32]{1,3,2,0:T(8,128)(2,1)} %get-tuple-element.327), kind=kOutput, calls=%fused_computation.2.clone.1 | convolution fusion | flops 553615360 | bytes 44433408 | tf_op jit(solution)/shard_map/while/body/eval_jaxpr/abhe,akhe->abhk/dot_general | solution.py:40
  417.5 15.6 %fusion.68 = f32[128,64,4]{1,2,0:T(4,128)S(1)} fusion(f32[128,4,256,64]{2,3,1,0:T(8,128)} %get-tuple-element.292, f32[128,64,4]{1,2,0:T(4,128)S(1)} %select_maximum_fusion.2, f32[64,4,256]{2,0,1:T(8,128)S(1)} %dynamic-slice_convert_fusion.2), kind=kLoop, calls=%fused_computation.4.clone.1 | loop fusion | flops 25133056 | bytes 34078720 | tf_op jit(solution)/shard_map/while/body/eval_jaxpr/reduce_sum | solution.py:45
  433.4 22.5 %bitcast_add_fusion.3 = f32[128,64,4,32]{1,3,2,0:T(8,128)} fusion(f32[128,64,4,32]{1,3,2,0:T(8,128)} %get-tuple-element.311, f32[128,64,4]{1,2,0:T(4,128)S(1)} %get-tuple-element.294, pred[]{:T(512)S(6)} %compare.6, bf16[128,256,4,32]{1,3,2,0:T(8,128)(2,1)} %bitcast.67, f32[128,4,256,64]{2,3,1,0:T(8,128)} %get-tuple-element.292, ...), kind=kOutput, calls=%fused_computation.8.clone.1 | convolution fusion | flops 565182464 | bytes 50855936 | tf_op jit(solution)/shard_map/while/body/eval_jaxpr/abhk,akhe->abhe/dot_general | solution.py:46
  456.9 9.1 %fusion.70 = bf16[128,256,128]{1,2,0:T(8,128)(2,1)} fusion(bf16[128,1024,128]{2,1,0:T(8,128)(2,1)} %get-tuple-element.325, s32[]{:T(128)S(6)} %select_n.39, bf16[128,128]{0,1:T(8,128)(2,1)S(1)} %get-tuple-element.329), kind=kOutput, calls=%fused_computation.15.clone.1 | convolution fusion | flops 1077936128 | bytes 16809988 | tf_op jit(solution)/shard_map/while/body/eval_jaxpr/dot_general | solution.py:38
  465.9 5.7 fusion.66
  471.7 16.0 %fusion.67 = (f32[128,64,4]{1,2,0:T(4,128)S(1)}, f32[128,4,256,64]{2,3,1,0:T(8,128)}) fusion(f32[64,4,256]{2,0,1:T(8,128)S(1)} %dynamic-slice_convert_fusion.2, bf16[128,256,4,32]{1,3,2,0:T(8,128)(2,1)S(1)} %bitcast.68, bf16[128,64,4,32]{1,3,2,0:T(8,128)(2,1)} %get-tuple-element.327), kind=kOutput, calls=%fused_computation.2.clone.1 | convolution fusion | flops 553615360 | bytes 44433408 | tf_op jit(solution)/shard_map/while/body/eval_jaxpr/abhe,akhe->abhk/dot_general | solution.py:40
  487.8 15.6 %fusion.68 = f32[128,64,4]{1,2,0:T(4,128)S(1)} fusion(f32[128,4,256,64]{2,3,1,0:T(8,128)} %get-tuple-element.292, f32[128,64,4]{1,2,0:T(4,128)S(1)} %select_maximum_fusion.2, f32[64,4,256]{2,0,1:T(8,128)S(1)} %dynamic-slice_convert_fusion.2), kind=kLoop, calls=%fused_computation.4.clone.1 | loop fusion | flops 25133056 | bytes 34078720 | tf_op jit(solution)/shard_map/while/body/eval_jaxpr/reduce_sum | solution.py:45
  503.7 22.5 %bitcast_add_fusion.3 = f32[128,64,4,32]{1,3,2,0:T(8,128)} fusion(f32[128,64,4,32]{1,3,2,0:T(8,128)} %get-tuple-element.311, f32[128,64,4]{1,2,0:T(4,128)S(1)} %get-tuple-element.294, pred[]{:T(512)S(6)} %compare.6, bf16[128,256,4,32]{1,3,2,0:T(8,128)(2,1)} %bitcast.67, f32[128,4,256,64]{2,3,1,0:T(8,128)} %get-tuple-element.292, ...), kind=kOutput, calls=%fused_computation.8.clone.1 | convolution fusion | flops 565182464 | bytes 50855936 | tf_op jit(solution)/shard_map/while/body/eval_jaxpr/abhk,akhe->abhe/dot_general | solution.py:46
  527.2 9.1 %fusion.70 = bf16[128,256,128]{1,2,0:T(8,128)(2,1)} fusion(bf16[128,1024,128]{2,1,0:T(8,128)(2,1)} %get-tuple-element.325, s32[]{:T(128)S(6)} %select_n.39, bf16[128,128]{0,1:T(8,128)(2,1)S(1)} %get-tuple-element.329), kind=kOutput, calls=%fused_computation.15.clone.1 | convolution fusion | flops 1077936128 | bytes 16809988 | tf_op jit(solution)/shard_map/while/body/eval_jaxpr/dot_general | solution.py:38
  536.2 5.7 fusion.66
  542.0 16.0 %fusion.67 = (f32[128,64,4]{1,2,0:T(4,128)S(1)}, f32[128,4,256,64]{2,3,1,0:T(8,128)}) fusion(f32[64,4,256]{2,0,1:T(8,128)S(1)} %dynamic-slice_convert_fusion.2, bf16[128,256,4,32]{1,3,2,0:T(8,128)(2,1)S(1)} %bitcast.68, bf16[128,64,4,32]{1,3,2,0:T(8,128)(2,1)} %get-tuple-element.327), kind=kOutput, calls=%fused_computation.2.clone.1 | convolution fusion | flops 553615360 | bytes 44433408 | tf_op jit(solution)/shard_map/while/body/eval_jaxpr/abhe,akhe->abhk/dot_general | solution.py:40
  558.0 15.6 %fusion.68 = f32[128,64,4]{1,2,0:T(4,128)S(1)} fusion(f32[128,4,256,64]{2,3,1,0:T(8,128)} %get-tuple-element.292, f32[128,64,4]{1,2,0:T(4,128)S(1)} %select_maximum_fusion.2, f32[64,4,256]{2,0,1:T(8,128)S(1)} %dynamic-slice_convert_fusion.2), kind=kLoop, calls=%fused_computation.4.clone.1 | loop fusion | flops 25133056 | bytes 34078720 | tf_op jit(solution)/shard_map/while/body/eval_jaxpr/reduce_sum | solution.py:45
  574.0 22.5 %bitcast_add_fusion.3 = f32[128,64,4,32]{1,3,2,0:T(8,128)} fusion(f32[128,64,4,32]{1,3,2,0:T(8,128)} %get-tuple-element.311, f32[128,64,4]{1,2,0:T(4,128)S(1)} %get-tuple-element.294, pred[]{:T(512)S(6)} %compare.6, bf16[128,256,4,32]{1,3,2,0:T(8,128)(2,1)} %bitcast.67, f32[128,4,256,64]{2,3,1,0:T(8,128)} %get-tuple-element.292, ...), kind=kOutput, calls=%fused_computation.8.clone.1 | convolution fusion | flops 565182464 | bytes 50855936 | tf_op jit(solution)/shard_map/while/body/eval_jaxpr/abhk,akhe->abhe/dot_general | solution.py:46
  596.7 8.6 %broadcast_divide_fusion = f32[128,64,4,32]{1,3,2,0:T(8,128)} fusion(f32[128,64,4,32]{1,3,2,0:T(8,128)} %get-tuple-element.160, f32[128,64,4]{1,2,0:T(4,128)S(1)} %get-tuple-element.161), kind=kLoop, calls=%fused_computation.33 | loop fusion | flops 1048576 | bytes 8519680 | tf_op jit(solution)/shard_map/div | solution.py:68
  605.4 7.5 %copy.25 = f32[128,64,128]{2,0,1:T(8,128)} copy(f32[128,64,128]{1,2,0:T(8,128)} %bitcast.69) | data formatting | bytes 8388608 | tf_op jit(solution)/shard_map/reshape | solution.py:69
  612.9 6.3 fusion.30
  619.1 4.3 copy.26
  (52 shorter events, 17.1 us)
Async XLA Ops:
  6.5 53.3 %copy-start = (bf16[128,128]{1,0:T(8,128)(2,1)S(1)}, bf16[128,128]{1,0:T(8,128)(2,1)}, u32[]{:S(2)}) copy-start(bf16[128,128]{1,0:T(8,128)(2,1)} %param.12) | copy-start | bytes 98308
  6.5 12.2 %copy-start.6 = (bf16[128,4]{0,1:T(4,128)(2,1)S(1)}, bf16[128,4]{0,1:T(4,128)(2,1)}, u32[]{:S(2)}) copy-start(bf16[128,4]{0,1:T(4,128)(2,1)} %param.16) | copy-start | bytes 3076
  6.5 53.0 %copy-start.4 = (bf16[128,128]{1,0:T(8,128)(2,1)S(1)}, bf16[128,128]{1,0:T(8,128)(2,1)}, u32[]{:S(2)}) copy-start(bf16[128,128]{1,0:T(8,128)(2,1)} %param.13) | copy-start | bytes 98308
  6.5 53.1 %copy-start.5 = (bf16[128,128]{1,0:T(8,128)(2,1)S(1)}, bf16[128,128]{1,0:T(8,128)(2,1)}, u32[]{:S(2)}) copy-start(bf16[128,128]{1,0:T(8,128)(2,1)} %param.14) | copy-start | bytes 98308
  6.5 49.2 %all-gather.5.cloned.1.call-start = ((), (), s32[]{:S(2)}) async-start(), calls=%async_computation.1 | async-start | bytes 1114112 | tf_op jit(solution)/shard_map/all_gather | solution.py:95
  18.8 40.1 %copy-start.2 = (bf16[128,64,128]{2,1,0:T(8,128)(2,1)}, bf16[128,64,128]{2,1,0:T(8,128)(2,1)S(1)}, u32[]{:S(2)}) copy-start(bf16[128,64,128]{2,1,0:T(8,128)(2,1)S(1)} %fusion.28) | copy-start | bytes 6291460
  21.3 117.0 %all-reduce.2.cloned.1.call-start = ((), (), s32[]{:S(2)}) async-start(), calls=%async_computation.2 | async-start | bytes 2097152 | tf_op jit(solution)/shard_map/psum | solution.py:11
  58.8 258.4 %all-gather.3.cloned.1.call-start = ((), (), s32[]{:S(2)}) async-start(), calls=%async_computation | async-start | bytes 35651584 | tf_op jit(solution)/shard_map/all_gather | solution.py:106
  605.4 7.5 %copy-start.3 = (bf16[128,64,128]{2,1,0:T(8,128)(2,1)S(1)}, bf16[128,64,128]{2,1,0:T(8,128)(2,1)}, u32[]{:S(2)}) copy-start(bf16[128,64,128]{2,1,0:T(8,128)(2,1)} %copy-done.2) | copy-start | bytes 6291460
  605.4 7.5 %copy-start.7 = (bf16[128,128]{1,0:T(8,128)(2,1)S(1)}, bf16[128,128]{1,0:T(8,128)(2,1)}, u32[]{:S(2)}) copy-start(bf16[128,128]{1,0:T(8,128)(2,1)} %param.17) | copy-start | bytes 98308
  605.4 7.5 %copy-start.8 = (bf16[128,128]{1,0:T(8,128)(2,1)S(1)}, bf16[128,128]{1,0:T(8,128)(2,1)}, u32[]{:S(2)}) copy-start(bf16[128,128]{1,0:T(8,128)(2,1)} %param.15) | copy-start | bytes 98308
  605.4 18.0 %copy-start.1 = (bf16[128,128]{1,0:T(8,128)(2,1)S(1)}, bf16[128,128]{1,0:T(8,128)(2,1)}, u32[]{:S(2)}) copy-start(bf16[128,128]{1,0:T(8,128)(2,1)} %param.12) | copy-start | bytes 98308
Sparse Core Ops, SparseCore 0:
  21.4 34.3 all-gather.4
  58.9 79.3 all-reduce.1
  139.9 177.2 all-gather.2
where the time goes:
time: 633 us; the launch traced here: 630 us
  waiting for transfers between devices  279 us (44%)
  matrix products  222 us (35%)
  other arithmetic  91.8 us (15%)
  local copies, waits for them, and re-layouts  23 us (4%)
  between operations  13.3 us (2%)
    all_gather x1, waiting for transfers between devices, shards(): lax.all_gather(normed, 'col', axis=1, tiled=True)  177 us
    dot_general x4, matrix products, absorb(): jnp.einsum('abhk,akhe->abhe', weights.astype(jnp.bfloat16), values, prefe...  87.9 us
    psum x1, waiting for transfers between devices, from_root(): return lax.psum(jnp.where(mine, value, jnp.zeros_like(value)), axis)  67.1 us
    dot_general x4, matrix products, absorb(): jnp.einsum('abhe,akhe->abhk', query, keys, preferred_element_type=jnp.flo...  63.9 us
    reduce_sum x4, other arithmetic, absorb(): total = total * factor + jnp.sum(weights, axis=-1)  62.6 us
    dot_general x4, matrix products, absorb(): jnp.dot(key_rows, w_value, preferred_element_type=jnp.float32)  36.2 us
    all_gather x1, waiting for transfers between devices, shards(): band = lax.all_gather(tile_bias, 'col', axis=2, tiled=True)  34.4 us
    dot_general x4, matrix products, absorb(): jnp.dot(key_rows, w_key, preferred_element_type=jnp.float32)  23 us
  transfers between devices with their start and end apart: 3, of which 3 were waited for; matrix products, arithmetic and copies ran while one was open for 2% of the time, Pallas kernels for 0%

commit v1 on v0

v1 whole, which is shorter than its diff:
```python
import math

import jax
import jax.numpy as jnp
from jax import lax
from jax.experimental import pallas as pl
from jax.experimental.pallas import tpu as pltpu
from jax.sharding import PartitionSpec as P

F32 = jnp.float32
BF16 = jnp.bfloat16
MESH = pl.DeviceIdType.MESH

HEADS = 4
HEAD_DIM = 32
D = 128
RES = 1024
ROWS, COLS = 8, 16
BAND = RES // ROWS
KEYS = RES // COLS
MINE = BAND // COLS
SLOTS = 8
HALF = RES // 2
PARTS = 4
KC = RES // PARTS
RC = HALF // PARTS


def layer_norm(tile, gain):
    values = tile.astype(F32)
    center = jnp.mean(values, axis=-1, keepdims=True)
    offset = values - center
    spread = jnp.mean(offset * offset, axis=-1, keepdims=True)
    return offset * lax.rsqrt(spread + 1e-05) * gain


def remote(src, dst, send, recv, row, col):
    return pltpu.make_async_remote_copy(
        src_ref=src, dst_ref=dst, send_sem=send, recv_sem=recv,
        device_id={"row": row, "col": col}, device_id_type=MESH,
    )


def kernel(
    x_ref, gain_ref, wq_ref, wk_ref, wv_ref, wg_ref, wb_ref, wo_ref, o_ref,
    got, piece_f, piece, bands, bias, w_all, q_s, k_s, v_s, g_s, s_s, p_s, acc_s, out_s,
    x_send, x_recv, x_own, b_send, b_recv, b_own, r_send, r_recv, c_send, c_recv, o_send, o_recv, o_own,
):
    row, col = lax.axis_index("row"), lax.axis_index("col")
    zh, y, core = row // 4, row % 4, col % 2
    row_z = (1 - zh) * 4 + y
    row_1 = zh * 4 + y + 1 - 2 * (y % 2)
    row_3 = zh * 4 + 3 - y
    col_c = col + 1 - 2 * core

    barrier = pltpu.get_barrier_semaphore()
    for d in range(1, COLS):
        pl.semaphore_signal(barrier, inc=1, device_id={"row": row, "col": (col + d) % COLS}, device_id_type=MESH)
    for other in (row_z, row_1, row_3):
        pl.semaphore_signal(barrier, inc=1, device_id={"row": other, "col": col}, device_id_type=MESH)
    pl.semaphore_wait(barrier, COLS - 1 + 3)

    own_keys = pl.ds(pl.multiple_of(col * KEYS, KEYS), KEYS)
    x_copies = []
    for part in range(2):
        for d in range(1, COLS):
            to = (col + d) % COLS
            copy = remote(
                x_ref.at[pl.ds(to * MINE + part * 4, 4)], got.at[pl.ds(part * 4, 4), own_keys],
                x_send.at[part, d], x_recv.at[part, d], row, to,
            )
            copy.start()
            x_copies.append(copy)
    x_local = pltpu.make_async_copy(x_ref.at[pl.ds(col * MINE, MINE)], got.at[:, own_keys], x_own)
    x_local.start()

    gain = gain_ref[...]

    @pl.loop(0, 8)
    def _(i):
        tile = x_ref[pl.ds(i * 16, 16)].reshape(16 * KEYS, D)
        g_s[pl.ds(pl.multiple_of(i * 16 * KEYS, 16 * KEYS), 16 * KEYS)] = layer_norm(tile, gain)

    @pl.loop(0, KEYS, unroll=8)
    def _(k):
        normed = g_s[pl.ds(k, BAND, stride=KEYS), :].astype(BF16)
        out = lax.dot_general(wb_ref[...], normed, (((1,), (1,)), ((), ())), preferred_element_type=F32)
        for h in range(HEADS):
            piece_f[h, pl.ds(k, 1)] = out[h : h + 1]

    piece[...] = piece_f[...].astype(BF16)

    b_copies = []
    for d in range(1, COLS):
        to = (col + d) % COLS
        heads = pl.ds((to % 2) * 2, 2)
        copy = remote(piece.at[heads], bands.at[0, heads, own_keys], b_send.at[d], b_recv.at[d], row, to)
        copy.start()
        b_copies.append(copy)
    mine = pl.ds(core * 2, 2)
    b_local = pltpu.make_async_copy(piece.at[mine], bands.at[0, mine, own_keys], b_own)
    b_local.start()

    w_all[:, 0:128] = wq_ref[...]
    w_all[:, 128:256] = wk_ref[...]
    w_all[:, 256:384] = wv_ref[...]
    w_all[:, 384:512] = wg_ref[...]
    v_s[:, :, 128:] = jnp.ones((MINE, RES, 128), BF16)
    p_s[1] = jnp.ones((HALF, RES), BF16)

    b_local.wait()
    for copy in b_copies:
        copy.wait_recv()

    def band(slot):
        return bands.at[slot, mine]

    def relay(src, dst, to_row, index):
        return remote(band(src), band(dst), r_send.at[index], r_recv.at[dst], to_row, col)

    def share(slot):
        return remote(band(slot), band(slot), c_send.at[slot], c_recv.at[slot], row, col_c)

    relays = [
        relay(0, 1, row_z, 0), relay(0, 2, row_1, 1), relay(0, 4, row_3, 2),
        relay(1, 3, row_1, 3), relay(1, 5, row_3, 4),
        relay(3, 7, row_3, 5), relay(4, 6, row_1, 6),
    ]
    shares = [share(slot) for slot in range(SLOTS)]
    landed = {1: relays[0], 2: relays[1], 3: relays[3], 4: relays[2], 5: relays[4], 6: relays[6], 7: relays[5]}

    relays[0].start()
    relays[1].start()
    relays[2].start()
    shares[0].start()

    lane = lax.broadcasted_iota(jnp.int32, (1, D), 1)
    own_lanes = [(lane >= HEAD_DIM * h) & (lane < HEAD_DIM * (h + 1)) for h in range(HEADS)]

    def slot_of(band_row):
        z, w = band_row // 4, band_row % 4
        odd, high = (w + y) % 2, (w // 2 + y // 2) % 2
        return (z + zh) % 2 + 2 * (2 * high + (odd + high) % 2)

    def project(first):
        @pl.loop(first, first + 4)
        def _(a):
            normed = layer_norm(got[a], gain).astype(BF16)
            mixed = jnp.dot(normed, w_all[...], preferred_element_type=F32)
            query = (mixed[:, 0:128] * (1.0 / math.sqrt(HEAD_DIM))).astype(BF16)
            k_s[a] = mixed[:, 128:256].astype(BF16)
            v_s[a, :, 0:128] = mixed[:, 256:384].astype(BF16)
            gate = jax.nn.sigmoid(mixed[:, 384:512])
            for r in range(ROWS):
                begin = pl.multiple_of(slot_of(r) * BAND, BAND)
                part = query[r * BAND : (r + 1) * BAND]
                for h in range(HEADS):
                    q_s[a, h, pl.ds(begin, BAND)] = jnp.where(own_lanes[h], part, jnp.zeros_like(part))
                g_s[pl.ds(pl.multiple_of(a * RES + begin, BAND), BAND)] = gate[r * BAND : (r + 1) * BAND]

    x_local.wait()
    for copy in x_copies[: COLS - 1]:
        copy.wait_recv()
    project(0)

    landed[1].wait_recv()
    relays[3].start()
    relays[4].start()
    shares[1].start()

    for copy in x_copies[COLS - 1 :]:
        copy.wait_recv()
    project(4)

    landed[2].wait_recv()
    shares[2].start()
    landed[4].wait_recv()
    relays[6].start()
    shares[4].start()
    landed[3].wait_recv()
    relays[5].start()
    shares[3].start()

    def take_bias(phase):
        for slot in range(4):
            shares[phase * 4 + slot].wait_recv()

        @pl.loop(0, HEADS)
        def _(h):
            for slot in range(4):
                for j in range(RES // 128):
                    block = bands[phase * 4 + slot, h, j * 128 : (j + 1) * 128].astype(F32)
                    bias[h, slot * BAND : (slot + 1) * BAND, j * 128 : (j + 1) * 128] = block.T

    def scores(step, h, j):
        phase, a = step // MINE, step % MINE
        rows = pl.ds(pl.multiple_of(phase * HALF, HALF), HALF)
        s_s[h % 2, :, j * KC : (j + 1) * KC] = lax.dot_general(
            q_s[a, h, rows], k_s[a, j * KC : (j + 1) * KC], (((1,), (1,)), ((), ())), preferred_element_type=F32
        )

    def soften(h, j):
        rows = slice(j * RC, (j + 1) * RC)
        logits = s_s[h % 2, rows] + bias[h, rows]
        most = jnp.max(logits, axis=-1, keepdims=True)
        p_s[h % 2, rows] = jnp.exp(logits - most).astype(BF16)

    def attend(step, h, j, total):
        a = step % MINE
        part = jnp.dot(
            p_s[h % 2, :, j * KC : (j + 1) * KC], v_s[a, j * KC : (j + 1) * KC], preferred_element_type=F32
        )
        return part if total is None else total + part

    def settle(total, h):
        head = total[:, 0:128] / total[:, 128:256]
        acc_s[...] = head if h == 0 else jnp.where(own_lanes[h], head, acc_s[...])

    def produce(step):
        phase, a = step // MINE, step % MINE
        begin = pl.multiple_of(phase * HALF, HALF)
        gate = g_s[pl.ds(pl.multiple_of(a * RES + begin, HALF), HALF)]
        gated = (gate * acc_s[...]).astype(BF16)
        out_s[a, pl.ds(begin, HALF)] = jnp.dot(gated, wo_ref[...], preferred_element_type=F32).astype(BF16)

    band_rows = [row, row_z, row_1, (1 - zh) * 4 + row_1 % 4, row_3, (1 - zh) * 4 + row_3 % 4,
                 zh * 4 + (y + 2) % 4, (1 - zh) * 4 + (y + 2) % 4]

    def deliver(step):
        phase, a = step // MINE, step % MINE
        for slot in range(4):
            owner = jnp.where(phase == 0, band_rows[slot], band_rows[slot + 4])
            for half in range(2):
                to = owner * 2 + half
                begin = pl.multiple_of((phase * 4 + slot) * BAND + half * KEYS, KEYS)
                src, dst = out_s.at[a, pl.ds(begin, KEYS)], o_ref.at[col * MINE + a]

                @pl.when(to != col)
                def _():
                    remote(src, dst, o_send.at[to], o_recv.at[col], row, to).start()

                @pl.when(to == col)
                def _():
                    pltpu.make_async_copy(src, dst, o_own).start()

    take_bias(0)
    for j in range(PARTS):
        scores(0, 0, j)

    @pl.loop(0, 2 * MINE)
    def _(step):
        before = (step + 2 * MINE - 1) % (2 * MINE)
        after = (step + 1) % (2 * MINE)

        @pl.when(step == 4)
        def _():
            for slot in (5, 6, 7):
                landed[slot].wait_recv()
                shares[slot].start()

        @pl.when(step == MINE)
        def _():
            take_bias(1)

        for h in range(HEADS):
            total = None
            for j in range(PARTS):
                if h < HEADS - 1:
                    scores(step, h + 1, j)
                else:
                    scores(after, 0, j)
                soften(h, j)
                total = attend(step if h else before, (h - 1) % HEADS, j, total)
            settle(total, (h - 1) % HEADS)
            if h == 0:
                produce(before)

        @pl.when(step > 0)
        def _():
            deliver(before)

    last = 2 * MINE - 1
    total = None
    for j in range(PARTS):
        total = attend(last, HEADS - 1, j, total)
    settle(total, HEADS - 1)
    produce(last)
    deliver(last)

    for copy in x_copies + b_copies + relays + shares:
        copy.wait_send()
    for d in range(1, COLS):
        other = (col + d) % COLS
        block = o_ref.at[pl.ds(other * MINE, MINE)]
        remote(block, block, o_send.at[other], o_recv.at[other], row, other).wait()
    block = o_ref.at[pl.ds(col * MINE, MINE)]
    pltpu.make_async_copy(block, block, o_own).wait()


def shards(pair, ln_gain, w_query, w_key, w_value, w_gate, w_bias, w_out):
    dma = pltpu.SemaphoreType.DMA
    vmem = pl.BlockSpec(memory_space=pltpu.VMEM)
    return pl.pallas_call(
        kernel,
        out_shape=jax.ShapeDtypeStruct(pair.shape, BF16),
        in_specs=[vmem] * 8,
        out_specs=pl.BlockSpec(memory_space=pl.ANY),
        scratch_shapes=[
            pltpu.VMEM((MINE, RES, D), BF16),
            pltpu.VMEM((HEADS, KEYS, BAND), F32),
            pltpu.VMEM((HEADS, KEYS, BAND), BF16),
            pltpu.VMEM((SLOTS, HEADS, RES, BAND), BF16),
            pltpu.VMEM((HEADS, HALF, RES), F32),
            pltpu.VMEM((D, 4 * D), BF16),
            pltpu.VMEM((MINE, HEADS, RES, D), BF16),
            pltpu.VMEM((MINE, RES, D), BF16),
            pltpu.VMEM((MINE, RES, 2 * D), BF16),
            pltpu.VMEM((MINE * RES, D), F32),
            pltpu.VMEM((2, HALF, RES), F32),
            pltpu.VMEM((2, HALF, RES), BF16),
            pltpu.VMEM((HALF, D), F32),
            pltpu.VMEM((MINE, RES, D), BF16),
            dma((2, COLS)), dma((2, COLS)), dma,
            dma((COLS,)), dma((COLS,)), dma,
            dma((7,)), dma((SLOTS,)),
            dma((SLOTS,)), dma((SLOTS,)),
            dma((COLS,)), dma((COLS,)), dma,
        ],
        compiler_params=pltpu.CompilerParams(
            collective_id=0, has_side_effects=True, vmem_limit_bytes=60 << 20
        ),
    )(
        pair, ln_gain.reshape(1, -1), w_query, w_key, w_value, w_gate,
        jnp.pad(w_bias.T, ((0, 8 - HEADS), (0, 0))), w_out,
    )


def solution(mesh):
    return jax.shard_map(
        shards,
        mesh=mesh,
        in_specs=(P("row", "col", None), P(), P(), P(), P(), P(), P(), P()),
        out_specs=P("row", "col", None),
        check_vma=False,
    )
```

time: 633 us -> 145 us (0.23)
  waiting for transfers between devices: 279 us -> 0 us
  matrix products: 222 us -> 0 us
  Pallas kernels: 0 us -> 140 us
  other arithmetic: 91.8 us -> 0 us
  local copies, waits for them, and re-layouts: 23 us -> 4.34 us
  between operations: 13.3 us -> 0.01 us
    dot_general x19 -> x0, matrix products: 222 us -> none  [the longest x4 87.9 us: absorb(): jnp.einsum('abhk,akhe->abhe', weights.astype(jnp.bfloat16), values, prefe...]
    all_gather x2 -> x0, waiting for transfers between devices: 211 us -> none  [the longest x1 177 us: shards(): lax.all_gather(normed, 'col', axis=1, tiled=True)]
    pallas_call x0 -> x1, Pallas kernels: none -> 140 us  [shards(): pl.pallas_call(kernel, out_shape=jax.ShapeDtypeStruct(pair.shape, BF16),...]
    reduce_sum x6 -> x0, other arithmetic: 69.4 us -> none  [the longest x4 62.6 us: absorb(): total = total * factor + jnp.sum(weights, axis=-1)]
    psum x1 -> x0, waiting for transfers between devices: 67.1 us -> none  [from_root(): return lax.psum(jnp.where(mine, value, jnp.zeros_like(value)), axis)]
    convert_element_type x5 -> x0, other arithmetic: 9.04 us -> none  [the longest x1 5.33 us: layer_norm(): ((values - center) * lax.rsqrt(spread + 1e-05) * gain).astype(jnp.bfloat16)]
    div x2 -> x0, other arithmetic: 8.65 us -> none  [the longest x1 8.64 us: finish(): attended = summed / total[..., None]]
    reshape x1 -> x0, local copies, waits for them, and re-layouts: 7.47 us -> none  [finish(): attended.reshape(attended.shape[0], attended.shape[1], attended.shape[2]...]
  transfers between devices with their start and end apart: 3 -> 0, of which waited for: 3 -> 0; matrix products, arithmetic and copies ran while one was open for 2% -> 0% of each run, Pallas kernels for 0% -> 0%
where the time goes in v1:
time: 145 us; the launch traced here: 144 us
  Pallas kernels  140 us (97%)
  local copies, waits for them, and re-layouts  4.34 us (3%)
    pallas_call x1, Pallas kernels, shards(): pl.pallas_call(kernel, out_shape=jax.ShapeDtypeStruct(pair.shape, BF16),...  140 us
    unnamed x1, local copies, waits for them, and re-layouts  3.08 us

profile of v1, /device:TPU:49, one launch (start us, length us, event | category | flops | bytes accessed | tf_op | source)
XLA Modules:
  0.0 144.0 jit_solution(8269043307416955353)
XLA Ops:
  0.0 1.3 pad.4.wb_ref
  1.3 139.6 %shard_map.82 = bf16[128,64,128]{2,1,0:T(8,128)(2,1)} custom-call(bf16[128,64,128]{2,1,0:T(8,128)(2,1)} %x_ref.1, f32[1,128]{1,0:T(1,128)} %bitcast.3, bf16[128,128]{1,0:T(8,128)(2,1)} %wq_ref.1, bf16[128,128]{1,0:T(8,128)(2,1)} %wk_ref.1, bf16[128,128]{1,0:T(8,128)(2,1)} %wv_ref.1, bf16[128,128]{1,0:T(8,128)(2,1)} %wg_ref.1, bf16[8,128]{1,0:T(8,128)(2,1)} %pad.4.wb_ref, ...), custom_call_target="tpu_custom_call" | custom-call | tf_op jit(solution)/shard_map/pallas_call | solution.py:303
  140.9 3.1 %copy.10 = bf16[128,64,128]{2,1,0:T(8,128)(2,1)} copy(bf16[128,64,128]{2,1,0:T(8,128)(2,1)} %shard_map.82) | data formatting | bytes 4194304

commit v2 on v1

v2 whole, which is shorter than its diff:
```python
import math

import jax
import jax.numpy as jnp
from jax import lax
from jax.experimental import pallas as pl
from jax.experimental.pallas import tpu as pltpu
from jax.sharding import PartitionSpec as P

F32 = jnp.float32
BF16 = jnp.bfloat16
MESH = pl.DeviceIdType.MESH

HEADS = 4
HEAD_DIM = 32
D = 128
RES = 1024
ROWS, COLS = 8, 16
BAND = RES // ROWS
KEYS = RES // COLS
MINE = BAND // COLS
SLOTS = 8
HALF = RES // 2
PARTS = 4
KC = RES // PARTS
RC = HALF // PARTS
ROW_PARTS = [(0, 3), (3, 2), (5, 2), (7, 1)]
ORDER = [
    (1, 2, 0), (0, 1, 0), (1, 0, 0), (0, 3, 0), (1, 1, 0), (0, 2, 0), (1, 3, 0),
    (1, 2, 1), (0, 1, 1), (1, 0, 1), (0, 3, 1), (1, 1, 1), (0, 2, 1), (1, 3, 1), (0, 0, 1),
]


def layer_norm(tile, gain):
    values = tile.astype(F32)
    center = jnp.mean(values, axis=-1, keepdims=True)
    offset = values - center
    spread = jnp.mean(offset * offset, axis=-1, keepdims=True)
    return offset * lax.rsqrt(spread + 1e-05) * gain


def remote(src, dst, send, recv, row, col):
    return pltpu.make_async_remote_copy(
        src_ref=src, dst_ref=dst, send_sem=send, recv_sem=recv,
        device_id={"row": row, "col": col}, device_id_type=MESH,
    )


def kernel(
    x_ref, gain_ref, wq_ref, wk_ref, wv_ref, wg_ref, wb_ref, wo_ref, o_ref,
    got, piece_f, piece, bands, bias, w_all, q_s, k_s, v_s, g_s, s_s, p_s, m_s, acc_s, out_s,
    x_send, x_recv, x_own, b_send, b_recv, b_own, r_send, r_recv, c_send, c_recv, o_send, o_recv, o_own,
):
    row, col = lax.axis_index("row"), lax.axis_index("col")
    zh, y, core = row // 4, row % 4, col % 2
    row_z = (1 - zh) * 4 + y
    row_1 = zh * 4 + y + 1 - 2 * (y % 2)
    row_3 = zh * 4 + 3 - y
    col_c = col + 1 - 2 * core
    col_z = (col + 8) % COLS

    barrier = pltpu.get_barrier_semaphore()
    for d in range(1, COLS):
        pl.semaphore_signal(barrier, inc=1, device_id={"row": row, "col": (col + d) % COLS}, device_id_type=MESH)
    for other, at in ((row_z, col_z), (row_1, col), (row_3, col)):
        pl.semaphore_signal(barrier, inc=1, device_id={"row": other, "col": at}, device_id_type=MESH)
    pl.semaphore_wait(barrier, COLS - 1 + 3)

    own_keys = pl.ds(pl.multiple_of(col * KEYS, KEYS), KEYS)
    z_low, x_at = col // 8, (col // 2) % 4
    others = [
        ((z_low + dz) % 2) * 8 + ((x_at + dx) % 4) * 2 + (core + dc) % 2 for dz, dx, dc in ORDER
    ]

    def exchange(part):
        first, count = ROW_PARTS[part]
        return [
            remote(
                x_ref.at[pl.ds(to * MINE + first, count)], got.at[pl.ds(first, count), own_keys],
                x_send.at[part, index], x_recv.at[part, index], row, to,
            )
            for index, to in enumerate(others)
        ]

    x_copies = [exchange(part) for part in range(4)]
    for copy in x_copies[0]:
        copy.start()
    x_local = pltpu.make_async_copy(x_ref.at[pl.ds(col * MINE, MINE)], got.at[:, own_keys], x_own)
    x_local.start()

    gain = gain_ref[...]
    acc_s[0:D] = jnp.zeros((D, D), F32)
    acc_s[0:D, 0:HEADS] = wb_ref[...].astype(F32)
    w_bias = acc_s[0:D].T[0:8].astype(BF16)

    @pl.loop(0, 8)
    def _(i):
        tile = x_ref[pl.ds(i * 16, 16)].reshape(16 * KEYS, D)
        g_s[pl.ds(pl.multiple_of(i * 16 * KEYS, 16 * KEYS), 16 * KEYS)] = layer_norm(tile, gain)

    @pl.loop(0, KEYS, unroll=8)
    def _(k):
        normed = g_s[pl.ds(k, BAND, stride=KEYS), :].astype(BF16)
        out = lax.dot_general(w_bias, normed, (((1,), (1,)), ((), ())), preferred_element_type=F32)
        for h in range(HEADS):
            piece_f[h, pl.ds(k, 1)] = out[h : h + 1]

    piece[...] = piece_f[...].astype(BF16)

    b_copies = []
    for index, to in enumerate(others):
        heads = pl.ds((to % 2) * 2, 2)
        copy = remote(piece.at[heads], bands.at[0, heads, own_keys], b_send.at[index], b_recv.at[index], row, to)
        copy.start()
        b_copies.append(copy)
    mine = pl.ds(core * 2, 2)
    b_local = pltpu.make_async_copy(piece.at[mine], bands.at[0, mine, own_keys], b_own)
    b_local.start()

    w_all[:, 0:128] = wq_ref[...]
    w_all[:, 128:256] = wk_ref[...]
    w_all[:, 256:384] = wv_ref[...]
    w_all[:, 384:512] = wg_ref[...]
    v_s[:, :, 128:] = jnp.ones((MINE, RES, 128), BF16)
    p_s[1] = jnp.ones((HALF, RES), BF16)

    b_local.wait()
    for copy in b_copies:
        copy.wait_recv()

    def band(slot):
        return bands.at[slot, mine]

    def relay(src, dst, to_row, index, to_col=col):
        return remote(band(src), band(dst), r_send.at[index], r_recv.at[dst], to_row, to_col)

    def share(slot):
        return remote(band(slot), band(slot), c_send.at[slot], c_recv.at[slot], row, col_c)

    relays = {
        1: relay(0, 1, row_z, 0, col_z), 2: relay(0, 2, row_1, 1), 3: relay(0, 3, row_3, 2),
        4: relay(1, 4, row_1, 3), 5: relay(1, 5, row_3, 4), 6: relay(3, 6, row_1, 5), 7: relay(4, 7, row_3, 6),
    }
    shares = [share(slot) for slot in range(SLOTS)]

    def arrive(slot, *onward):
        relays[slot].wait_recv()
        for then in onward:
            relays[then].start()
        shares[slot].start()

    for slot in (1, 2, 3):
        relays[slot].start()
    shares[0].start()
    for part in (1, 2, 3):
        for copy in x_copies[part]:
            copy.start()

    lane = lax.broadcasted_iota(jnp.int32, (1, D), 1)
    own_lanes = [(lane >= HEAD_DIM * h) & (lane < HEAD_DIM * (h + 1)) for h in range(HEADS)]

    def slot_of(band_row):
        z, w = band_row // 4, band_row % 4
        far, odd, high = (z + zh) % 2, (w + y) % 2, (w // 2 + y // 2) % 2
        near = odd * (2 + high + 2 * far)
        return near + (1 - odd) * (far + 6 * high)

    def project(part):
        for copy in x_copies[part]:
            copy.wait_recv()

        first, count = ROW_PARTS[part]

        @pl.loop(first, first + count)
        def _(a):
            normed = layer_norm(got[a], gain).astype(BF16)
            mixed = jnp.dot(normed, w_all[...], preferred_element_type=F32)
            query = (mixed[:, 0:128] * (1.0 / math.sqrt(HEAD_DIM))).astype(BF16)
            k_s[a] = mixed[:, 128:256].astype(BF16)
            v_s[a, :, 0:128] = mixed[:, 256:384].astype(BF16)
            gate = jax.nn.sigmoid(mixed[:, 384:512])
            for r in range(ROWS):
                begin = pl.multiple_of(slot_of(r) * BAND, BAND)
                part = query[r * BAND : (r + 1) * BAND]
                for h in range(HEADS):
                    q_s[a, h, pl.ds(begin, BAND)] = jnp.where(own_lanes[h], part, jnp.zeros_like(part))
                g_s[pl.ds(pl.multiple_of(a * RES + begin, BAND), BAND)] = gate[r * BAND : (r + 1) * BAND]

    x_local.wait()
    project(0)

    def take(slot):
        shares[slot].wait_recv()
        begin = slot * BAND

        @pl.loop(0, HEADS)
        def _(h):
            for j in range(RES // 128):
                block = bands[slot, h, j * 128 : (j + 1) * 128].astype(F32)
                bias[h, begin : begin + BAND, j * 128 : (j + 1) * 128] = block.T

    arrive(1, 4, 5)
    arrive(2)
    arrive(3, 6)
    for slot in range(4):
        take(slot)

    def scores(step, h, j):
        phase, a = step // MINE, step % MINE
        rows = pl.ds(pl.multiple_of(phase * HALF, HALF), HALF)
        keys = slice(j * KC, (j + 1) * KC)
        logits = lax.dot_general(
            q_s[a, h, rows], k_s[a, keys], (((1,), (1,)), ((), ())), preferred_element_type=F32
        ) + bias[h, rows, keys]
        s_s[h % 2, :, keys] = logits
        most = logits[:, 0:128]
        for begin in range(128, KC, 128):
            most = jnp.maximum(most, logits[:, begin : begin + 128])
        m_s[h % 2] = most if j == 0 else jnp.maximum(m_s[h % 2], most)

    def soften(h, j):
        rows = slice(j * RC, (j + 1) * RC)
        most = jnp.max(m_s[h % 2, rows], axis=-1, keepdims=True)
        p_s[h % 2, rows] = jnp.exp(s_s[h % 2, rows] - most).astype(BF16)

    def attend(step, h):
        return jnp.dot(p_s[h % 2], v_s[step % MINE], preferred_element_type=F32)

    def settle(total, h):
        head = total[:, 0:128] / total[:, 128:256]
        acc_s[...] = head if h == 0 else jnp.where(own_lanes[h], head, acc_s[...])

    def produce(step):
        phase, a = step // MINE, step % MINE
        begin = pl.multiple_of(phase * HALF, HALF)
        gate = g_s[pl.ds(pl.multiple_of(a * RES + begin, HALF), HALF)]
        gated = (gate * acc_s[...]).astype(BF16)
        out_s[a, pl.ds(begin, HALF)] = jnp.dot(gated, wo_ref[...], preferred_element_type=F32).astype(BF16)

    band_rows = [row, row_z, row_1, row_3, (1 - zh) * 4 + row_1 % 4, (1 - zh) * 4 + row_3 % 4,
                 zh * 4 + (y + 2) % 4, (1 - zh) * 4 + (y + 2) % 4]

    def deliver(step):
        phase, a = step // MINE, step % MINE
        for slot in range(4):
            owner = jnp.where(phase == 0, band_rows[slot], band_rows[slot + 4])
            for half in range(2):
                to = owner * 2 + half
                begin = pl.multiple_of((phase * 4 + slot) * BAND + half * KEYS, KEYS)
                src, dst = out_s.at[a, pl.ds(begin, KEYS)], o_ref.at[col * MINE + a]

                @pl.when(to != col)
                def _():
                    remote(src, dst, o_send.at[to], o_recv.at[col], row, to).start()

                @pl.when(to == col)
                def _():
                    pltpu.make_async_copy(src, dst, o_own).start()

    for j in range(PARTS):
        scores(0, 0, j)

    steps = 2 * MINE

    @pl.loop(0, MINE)
    def _(turn):
        for part in (1, 2, 3):

            @pl.when(turn == part)
            def _():
                project(part)

        @pl.when(turn == 1)
        def _():
            arrive(4, 7)

        @pl.when(turn == 2)
        def _():
            arrive(5)
            arrive(6)

        @pl.when(turn == 3)
        def _():
            arrive(7)
            for slot in range(4, 8):
                take(slot)

        for index in range(2 * HEADS):
            h = index % HEADS
            step = turn * 2 + index // HEADS
            before, after = (step + steps - 1) % steps, (step + 1) % steps
            for j in range(PARTS):
                if h < HEADS - 1:
                    scores(step, h + 1, j)
                else:
                    scores(after, 0, j)
                soften(h, j)
                if j == 0:
                    total = attend(step if h else before, (h - 1) % HEADS)
            settle(total, (h - 1) % HEADS)
            if h == 0:
                produce(before)

        @pl.when(turn > 0)
        def _():
            deliver(turn * 2 - 1)

        deliver(turn * 2)

    last = steps - 1
    settle(attend(last, HEADS - 1), HEADS - 1)
    produce(last)
    deliver(last)

    for copy in sum(x_copies, []) + b_copies + list(relays.values()) + shares:
        copy.wait_send()
    for d in range(1, COLS):
        other = (col + d) % COLS
        block = o_ref.at[pl.ds(other * MINE, MINE)]
        remote(block, block, o_send.at[other], o_recv.at[other], row, other).wait()
    block = o_ref.at[pl.ds(col * MINE, MINE)]
    pltpu.make_async_copy(block, block, o_own).wait()


def shards(pair, ln_gain, w_query, w_key, w_value, w_gate, w_bias, w_out):
    dma = pltpu.SemaphoreType.DMA
    vmem = pl.BlockSpec(memory_space=pltpu.VMEM)
    return pl.pallas_call(
        kernel,
        out_shape=jax.ShapeDtypeStruct(pair.shape, BF16),
        in_specs=[vmem] * 8,
        out_specs=pl.BlockSpec(memory_space=pl.ANY),
        scratch_shapes=[
            pltpu.VMEM((MINE, RES, D), BF16),
            pltpu.VMEM((HEADS, KEYS, BAND), F32),
            pltpu.VMEM((HEADS, KEYS, BAND), BF16),
            pltpu.VMEM((SLOTS, HEADS, RES, BAND), BF16),
            pltpu.VMEM((HEADS, RES, RES), F32),
            pltpu.VMEM((D, 4 * D), BF16),
            pltpu.VMEM((MINE, HEADS, RES, D), BF16),
            pltpu.VMEM((MINE, RES, D), BF16),
            pltpu.VMEM((MINE, RES, 2 * D), BF16),
            pltpu.VMEM((MINE * RES, D), F32),
            pltpu.VMEM((2, HALF, RES), F32),
            pltpu.VMEM((2, HALF, RES), BF16),
            pltpu.VMEM((2, HALF, 128), F32),
            pltpu.VMEM((HALF, D), F32),
            pltpu.VMEM((MINE, RES, D), BF16),
            dma((4, COLS)), dma((4, COLS)), dma,
            dma((COLS,)), dma((COLS,)), dma,
            dma((7,)), dma((SLOTS,)),
            dma((SLOTS,)), dma((SLOTS,)),
            dma((COLS,)), dma((COLS,)), dma,
        ],
        compiler_params=pltpu.CompilerParams(
            collective_id=0, has_side_effects=True, vmem_limit_bytes=62 << 20
        ),
    )(
        pair, ln_gain.reshape(1, -1), w_query, w_key, w_value, w_gate, w_bias, w_out,
    )


def solution(mesh):
    return jax.shard_map(
        shards,
        mesh=mesh,
        in_specs=(P("row", "col", None), P(), P(), P(), P(), P(), P(), P()),
        out_specs=P("row", "col", None),
        check_vma=False,
    )
```

time: 145 us -> 118 us (0.81)
  Pallas kernels: 140 us -> 113 us
    pallas_call x1, Pallas kernels: 140 us -> 113 us  [shards(): pl.pallas_call(kernel, out_shape=jax.ShapeDtypeStruct(pair.shape, BF16),...]
    unnamed x1 -> x2, local copies, waits for them, and re-layouts: 3.08 us -> 4.49 us
where the time goes in v2:
time: 118 us; the launch traced here: 117 us
  Pallas kernels  113 us (96%)
  local copies, waits for them, and re-layouts  4.49 us (4%)
    pallas_call x1, Pallas kernels, shards(): pl.pallas_call(kernel, out_shape=jax.ShapeDtypeStruct(pair.shape, BF16),...  113 us
    unnamed x2, local copies, waits for them, and re-layouts  4.49 us

profile of v2, /device:TPU:49, one launch (start us, length us, event | category | flops | bytes accessed | tf_op | source)
XLA Modules:
  0.0 117.4 jit_solution(4846650834861962907)
XLA Ops:
  0.0 1.4 %copy.9.wb_ref = bf16[128,4]{1,0:T(8,128)(2,1)} copy(bf16[128,4]{0,1:T(4,128)(2,1)} %param.14) | data formatting | bytes 2048 | tf_op args[6]
  1.4 112.9 %shard_map.82 = bf16[128,64,128]{2,1,0:T(8,128)(2,1)} custom-call(bf16[128,64,128]{2,1,0:T(8,128)(2,1)} %x_ref.1, f32[1,128]{1,0:T(1,128)} %bitcast.1, bf16[128,128]{1,0:T(8,128)(2,1)} %wq_ref.1, bf16[128,128]{1,0:T(8,128)(2,1)} %wk_ref.1, bf16[128,128]{1,0:T(8,128)(2,1)} %wv_ref.1, bf16[128,128]{1,0:T(8,128)(2,1)} %wg_ref.1, bf16[128,4]{1,0:T(8,128)(2,1)} %copy.9.wb_ref, ...), custom_call_target="tpu_custom_call" | custom-call | tf_op jit(solution)/shard_map/pallas_call | solution.py:328
  114.3 3.1 %copy.11 = bf16[128,64,128]{2,1,0:T(8,128)(2,1)} copy(bf16[128,64,128]{2,1,0:T(8,128)(2,1)} %shard_map.82) | data formatting | bytes 4194304

commit v3 on v2

--- a/solution.py
+++ b/solution.py
@@ -24,7 +24,8 @@
 PARTS = 4
 KC = RES // PARTS
 RC = HALF // PARTS
-ROW_PARTS = [(0, 3), (3, 2), (5, 2), (7, 1)]
+SENT = [(0, 3), (3, 2), (5, 3)]
+PROJECTED = [(0, 3), (3, 2), (5, 2), (7, 1)]
 ORDER = [
     (1, 2, 0), (0, 1, 0), (1, 0, 0), (0, 3, 0), (1, 1, 0), (0, 2, 0), (1, 3, 0),
     (1, 2, 1), (0, 1, 1), (1, 0, 1), (0, 3, 1), (1, 1, 1), (0, 2, 1), (1, 3, 1), (0, 0, 1),
@@ -64,7 +65,6 @@
         pl.semaphore_signal(barrier, inc=1, device_id={"row": row, "col": (col + d) % COLS}, device_id_type=MESH)
     for other, at in ((row_z, col_z), (row_1, col), (row_3, col)):
         pl.semaphore_signal(barrier, inc=1, device_id={"row": other, "col": at}, device_id_type=MESH)
-    pl.semaphore_wait(barrier, COLS - 1 + 3)
 
     own_keys = pl.ds(pl.multiple_of(col * KEYS, KEYS), KEYS)
     z_low, x_at = col // 8, (col // 2) % 4
@@ -73,7 +73,7 @@
     ]
 
     def exchange(part):
-        first, count = ROW_PARTS[part]
+        first, count = SENT[part]
         return [
             remote(
                 x_ref.at[pl.ds(to * MINE + first, count)], got.at[pl.ds(first, count), own_keys],
@@ -82,16 +82,17 @@
             for index, to in enumerate(others)
         ]
 
-    x_copies = [exchange(part) for part in range(4)]
+    x_copies = [exchange(part) for part in range(3)]
+    gain = gain_ref[...]
+    acc_s[0:D] = jnp.zeros((D, D), F32)
+    acc_s[0:D, 0:HEADS] = wb_ref[...].astype(F32)
+    w_bias = acc_s[0:D].T[0:8].astype(BF16)
+
+    pl.semaphore_wait(barrier, COLS - 1 + 3)
     for copy in x_copies[0]:
         copy.start()
     x_local = pltpu.make_async_copy(x_ref.at[pl.ds(col * MINE, MINE)], got.at[:, own_keys], x_own)
     x_local.start()
-
-    gain = gain_ref[...]
-    acc_s[0:D] = jnp.zeros((D, D), F32)
-    acc_s[0:D, 0:HEADS] = wb_ref[...].astype(F32)
-    w_bias = acc_s[0:D].T[0:8].astype(BF16)
 
     @pl.loop(0, 8)
     def _(i):
@@ -131,30 +132,36 @@
     def band(slot):
         return bands.at[slot, mine]
 
-    def relay(src, dst, to_row, index, to_col=col):
-        return remote(band(src), band(dst), r_send.at[index], r_recv.at[dst], to_row, to_col)
+    def relay(src, dst, index, to_row, to_col=col, heads=mine):
+        return remote(
+            bands.at[src, heads], bands.at[dst, heads], r_send.at[index], r_recv.at[index], to_row, to_col
+        )
 
     def share(slot):
         return remote(band(slot), band(slot), c_send.at[slot], c_recv.at[slot], row, col_c)
 
     relays = {
-        1: relay(0, 1, row_z, 0, col_z), 2: relay(0, 2, row_1, 1), 3: relay(0, 3, row_3, 2),
-        4: relay(1, 4, row_1, 3), 5: relay(1, 5, row_3, 4), 6: relay(3, 6, row_1, 5), 7: relay(4, 7, row_3, 6),
+        1: [relay(0, 1, 1, row_z, col_z)], 2: [relay(0, 2, 2, row_1)], 3: [relay(0, 3, 3, row_3)],
+        4: [relay(1, 4, 4, row_1)], 5: [relay(3, 5, 5, row_z, col_z)], 6: [relay(2, 6, 6, row_3)],
+        7: [
+            relay(5, 7, 7, row_1, heads=pl.ds(core * 2, 1)),
+            relay(4, 7, 0, row_3, heads=pl.ds(core * 2 + 1, 1)),
+        ],
     }
     shares = [share(slot) for slot in range(SLOTS)]
 
-    def arrive(slot, *onward):
-        relays[slot].wait_recv()
-        for then in onward:
-            relays[then].start()
+    def arrive(slot, onward=None):
+        for copy in relays[slot]:
+            copy.wait_recv()
+        if onward is not None:
+            onward.start()
         shares[slot].start()
 
     for slot in (1, 2, 3):
-        relays[slot].start()
+        relays[slot][0].start()
     shares[0].start()
-    for part in (1, 2, 3):
-        for copy in x_copies[part]:
-            copy.start()
+    for copy in x_copies[1] + x_copies[2]:
+        copy.start()
 
     lane = lax.broadcasted_iota(jnp.int32, (1, D), 1)
     own_lanes = [(lane >= HEAD_DIM * h) & (lane < HEAD_DIM * (h + 1)) for h in range(HEADS)]
@@ -166,10 +173,10 @@
         return near + (1 - odd) * (far + 6 * high)
 
     def project(part):
-        for copy in x_copies[part]:
-            copy.wait_recv()
-
-        first, count = ROW_PARTS[part]
+        if part < 3:
+            for copy in x_copies[part]:
+                copy.wait_recv()
+        first, count = PROJECTED[part]
 
         @pl.loop(first, first + count)
         def _(a):
@@ -199,9 +206,9 @@
                 block = bands[slot, h, j * 128 : (j + 1) * 128].astype(F32)
                 bias[h, begin : begin + BAND, j * 128 : (j + 1) * 128] = block.T
 
-    arrive(1, 4, 5)
-    arrive(2)
-    arrive(3, 6)
+    arrive(1, relays[4][0])
+    arrive(2, relays[6][0])
+    arrive(3, relays[5][0])
     for slot in range(4):
         take(slot)
 
@@ -272,11 +279,11 @@
 
         @pl.when(turn == 1)
         def _():
-            arrive(4, 7)
+            arrive(4, relays[7][1])
+            arrive(5, relays[7][0])
 
         @pl.when(turn == 2)
         def _():
-            arrive(5)
             arrive(6)
 
         @pl.when(turn == 3)
@@ -312,7 +319,7 @@
     produce(last)
     deliver(last)
 
-    for copy in sum(x_copies, []) + b_copies + list(relays.values()) + shares:
+    for copy in sum(x_copies, []) + b_copies + sum(relays.values(), []) + shares:
         copy.wait_send()
     for d in range(1, COLS):
         other = (col + d) % COLS
@@ -346,9 +353,9 @@
             pltpu.VMEM((2, HALF, 128), F32),
             pltpu.VMEM((HALF, D), F32),
             pltpu.VMEM((MINE, RES, D), BF16),
-            dma((4, COLS)), dma((4, COLS)), dma,
+            dma((3, COLS)), dma((3, COLS)), dma,
             dma((COLS,)), dma((COLS,)), dma,
-            dma((7,)), dma((SLOTS,)),
+            dma((SLOTS,)), dma((SLOTS,)),
             dma((SLOTS,)), dma((SLOTS,)),
             dma((COLS,)), dma((COLS,)), dma,
         ],

time: 118 us -> 114 us (0.966)
  Pallas kernels: 113 us -> 109 us
    pallas_call x1, Pallas kernels: 113 us -> 109 us  [shards(): pl.pallas_call(kernel, out_shape=jax.ShapeDtypeStruct(pair.shape, BF16),...]
where the time goes in v3:
time: 114 us
  Pallas kernels  109 us (96%)
  local copies, waits for them, and re-layouts  4.49 us (4%)
    pallas_call x1, Pallas kernels, shards(): pl.pallas_call(kernel, out_shape=jax.ShapeDtypeStruct(pair.shape, BF16),...  109 us
    unnamed x2, local copies, waits for them, and re-layouts  4.49 us

profile of v3, /device:TPU:49, one launch (start us, length us, event | category | flops | bytes accessed | tf_op | source)
XLA Modules:
  0.0 113.6 jit_solution(16173002816751778106)
XLA Ops:
  0.0 1.4 %copy.9.wb_ref = bf16[128,4]{1,0:T(8,128)(2,1)} copy(bf16[128,4]{0,1:T(4,128)(2,1)} %param.14) | data formatting | bytes 2048 | tf_op args[6]
  1.4 109.1 %shard_map.82 = bf16[128,64,128]{2,1,0:T(8,128)(2,1)} custom-call(bf16[128,64,128]{2,1,0:T(8,128)(2,1)} %x_ref.1, f32[1,128]{1,0:T(1,128)} %bitcast.1, bf16[128,128]{1,0:T(8,128)(2,1)} %wq_ref.1, bf16[128,128]{1,0:T(8,128)(2,1)} %wk_ref.1, bf16[128,128]{1,0:T(8,128)(2,1)} %wv_ref.1, bf16[128,128]{1,0:T(8,128)(2,1)} %wg_ref.1, bf16[128,4]{1,0:T(8,128)(2,1)} %copy.9.wb_ref, ...), custom_call_target="tpu_custom_call" | custom-call | tf_op jit(solution)/shard_map/pallas_call | solution.py:335
  110.5 3.1 %copy.11 = bf16[128,64,128]{2,1,0:T(8,128)(2,1)} copy(bf16[128,64,128]{2,1,0:T(8,128)(2,1)} %shard_map.82) | data formatting | bytes 4194304

commit v4 on v3

--- a/solution.py
+++ b/solution.py
@@ -94,12 +94,12 @@
     x_local = pltpu.make_async_copy(x_ref.at[pl.ds(col * MINE, MINE)], got.at[:, own_keys], x_own)
     x_local.start()
 
-    @pl.loop(0, 8)
+    @pl.loop(0, 8, unroll=2)
     def _(i):
         tile = x_ref[pl.ds(i * 16, 16)].reshape(16 * KEYS, D)
         g_s[pl.ds(pl.multiple_of(i * 16 * KEYS, 16 * KEYS), 16 * KEYS)] = layer_norm(tile, gain)
 
-    @pl.loop(0, KEYS, unroll=8)
+    @pl.loop(0, KEYS, unroll=16)
     def _(k):
         normed = g_s[pl.ds(k, BAND, stride=KEYS), :].astype(BF16)
         out = lax.dot_general(w_bias, normed, (((1,), (1,)), ((), ())), preferred_element_type=F32)
@@ -108,12 +108,18 @@
 
     piece[...] = piece_f[...].astype(BF16)
 
-    b_copies = []
-    for index, to in enumerate(others):
-        heads = pl.ds((to % 2) * 2, 2)
-        copy = remote(piece.at[heads], bands.at[0, heads, own_keys], b_send.at[index], b_recv.at[index], row, to)
+    b_copies = [
+        [
+            remote(
+                piece.at[pl.ds((to % 2) * 2 + part, 1)], bands.at[0, pl.ds((to % 2) * 2 + part, 1), own_keys],
+                b_send.at[part, index], b_recv.at[part, index], row, to,
+            )
+            for index, to in enumerate(others)
+        ]
+        for part in range(2)
+    ]
+    for copy in b_copies[0] + b_copies[1]:
         copy.start()
-        b_copies.append(copy)
     mine = pl.ds(core * 2, 2)
     b_local = pltpu.make_async_copy(piece.at[mine], bands.at[0, mine, own_keys], b_own)
     b_local.start()
@@ -125,27 +131,24 @@
     v_s[:, :, 128:] = jnp.ones((MINE, RES, 128), BF16)
     p_s[1] = jnp.ones((HALF, RES), BF16)
 
-    b_local.wait()
-    for copy in b_copies:
-        copy.wait_recv()
-
-    def band(slot):
-        return bands.at[slot, mine]
-
     def relay(src, dst, index, to_row, to_col=col, heads=mine):
         return remote(
             bands.at[src, heads], bands.at[dst, heads], r_send.at[index], r_recv.at[index], to_row, to_col
         )
 
     def share(slot):
-        return remote(band(slot), band(slot), c_send.at[slot], c_recv.at[slot], row, col_c)
-
+        band = bands.at[slot, mine]
+        return remote(band, band, c_send.at[slot], c_recv.at[slot], row, col_c)
+
+    single = [pl.ds(core * 2 + part, 1) for part in range(2)]
     relays = {
-        1: [relay(0, 1, 1, row_z, col_z)], 2: [relay(0, 2, 2, row_1)], 3: [relay(0, 3, 3, row_3)],
+        1: [relay(0, 1, part, row_z, col_z, single[part]) for part in range(2)],
+        2: [relay(0, 2, 2 + part, row_1, col, single[part]) for part in range(2)],
+        3: [relay(0, 3, 8 + part, row_3, col, single[part]) for part in range(2)],
         4: [relay(1, 4, 4, row_1)], 5: [relay(3, 5, 5, row_z, col_z)], 6: [relay(2, 6, 6, row_3)],
         7: [
-            relay(5, 7, 7, row_1, heads=pl.ds(core * 2, 1)),
-            relay(4, 7, 0, row_3, heads=pl.ds(core * 2 + 1, 1)),
+            relay(5, 7, 7, row_1, heads=single[0]),
+            relay(4, 7, 10, row_3, heads=single[1]),
         ],
     }
     shares = [share(slot) for slot in range(SLOTS)]
@@ -157,8 +160,12 @@
             onward.start()
         shares[slot].start()
 
-    for slot in (1, 2, 3):
-        relays[slot][0].start()
+    b_local.wait()
+    for part in range(2):
+        for copy in b_copies[part]:
+            copy.wait_recv()
+        for slot in (1, 2, 3):
+            relays[slot][part].start()
     shares[0].start()
     for copy in x_copies[1] + x_copies[2]:
         copy.start()
@@ -194,8 +201,6 @@
                 g_s[pl.ds(pl.multiple_of(a * RES + begin, BAND), BAND)] = gate[r * BAND : (r + 1) * BAND]
 
     x_local.wait()
-    project(0)
-
     def take(slot):
         shares[slot].wait_recv()
         begin = slot * BAND
@@ -206,10 +211,13 @@
                 block = bands[slot, h, j * 128 : (j + 1) * 128].astype(F32)
                 bias[h, begin : begin + BAND, j * 128 : (j + 1) * 128] = block.T
 
+    project(0)
+    take(0)
+
     arrive(1, relays[4][0])
     arrive(2, relays[6][0])
     arrive(3, relays[5][0])
-    for slot in range(4):
+    for slot in (1, 2, 3):
         take(slot)
 
     def scores(step, h, j):
@@ -277,13 +285,10 @@
             def _():
                 project(part)
 
-        @pl.when(turn == 1)
+        @pl.when(turn == 2)
         def _():
             arrive(4, relays[7][1])
             arrive(5, relays[7][0])
-
-        @pl.when(turn == 2)
-        def _():
             arrive(6)
 
         @pl.when(turn == 3)
@@ -319,7 +324,7 @@
     produce(last)
     deliver(last)
 
-    for copy in sum(x_copies, []) + b_copies + sum(relays.values(), []) + shares:
+    for copy in sum(x_copies, []) + sum(b_copies, []) + sum(relays.values(), []) + shares:
         copy.wait_send()
     for d in range(1, COLS):
         other = (col + d) % COLS
@@ -354,8 +359,8 @@
             pltpu.VMEM((HALF, D), F32),
             pltpu.VMEM((MINE, RES, D), BF16),
             dma((3, COLS)), dma((3, COLS)), dma,
-            dma((COLS,)), dma((COLS,)), dma,
-            dma((SLOTS,)), dma((SLOTS,)),
+            dma((2, COLS)), dma((2, COLS)), dma,
+            dma((11,)), dma((11,)),
             dma((SLOTS,)), dma((SLOTS,)),
             dma((COLS,)), dma((COLS,)), dma,
         ],

time: 114 us -> 111 us (0.974)
  Pallas kernels: 109 us -> 107 us
    pallas_call x1, Pallas kernels: 109 us -> 107 us  [shards(): pl.pallas_call(kernel, out_shape=jax.ShapeDtypeStruct(pair.shape, BF16),...]
where the time goes in v4:
time: 111 us
  Pallas kernels  107 us (96%)
  local copies, waits for them, and re-layouts  4.49 us (4%)
    pallas_call x1, Pallas kernels, shards(): pl.pallas_call(kernel, out_shape=jax.ShapeDtypeStruct(pair.shape, BF16),...  107 us
    unnamed x2, local copies, waits for them, and re-layouts  4.49 us

profile of v4, /device:TPU:49, one launch (start us, length us, event | category | flops | bytes accessed | tf_op | source)
XLA Modules:
  0.0 111.2 jit_solution(14886517649622263742)
XLA Ops:
  0.0 1.4 %copy.9.wb_ref = bf16[128,4]{1,0:T(8,128)(2,1)} copy(bf16[128,4]{0,1:T(4,128)(2,1)} %param.14) | data formatting | bytes 2048 | tf_op args[6]
  1.4 106.7 %shard_map.82 = bf16[128,64,128]{2,1,0:T(8,128)(2,1)} custom-call(bf16[128,64,128]{2,1,0:T(8,128)(2,1)} %x_ref.1, f32[1,128]{1,0:T(1,128)} %bitcast.1, bf16[128,128]{1,0:T(8,128)(2,1)} %wq_ref.1, bf16[128,128]{1,0:T(8,128)(2,1)} %wk_ref.1, bf16[128,128]{1,0:T(8,128)(2,1)} %wv_ref.1, bf16[128,128]{1,0:T(8,128)(2,1)} %wg_ref.1, bf16[128,4]{1,0:T(8,128)(2,1)} %copy.9.wb_ref, ...), custom_call_target="tpu_custom_call" | custom-call | tf_op jit(solution)/shard_map/pallas_call | solution.py:340
  108.2 3.1 %copy.11 = bf16[128,64,128]{2,1,0:T(8,128)(2,1)} copy(bf16[128,64,128]{2,1,0:T(8,128)(2,1)} %shard_map.82) | data formatting | bytes 4194304
